TPU v7x, 32 devices: a whole 2x2x4 slice. The times are simulated.
32 devices in a mesh: span: 16 (over z, x, core), chord: 2 (over y).
Axes of the slice: x: 2, y: 2, z: 4, core: 2. Of those that a mesh axis runs over, the one named last changes fastest.
Arguments:
- adjoint_flow: float32 [5, 16, 128, 256], P(None, None, 'span', 'chord'), may hold values from -6 to 6
- flow_grad: float32 [5, 16, 128, 256], P(None, None, 'span', 'chord'), may hold values from -6 to 6
- diagonal: float32 [16, 128, 256], P(None, 'span', 'chord'), may hold values from 4 to 6
- couplings: float32 [3, 16, 128, 256], P(None, None, 'span', 'chord'), may hold values from 0.3 to 1.5
- upwind: float32 [3, 5, 5], replicated, may hold values from -2.5 to 2.5
- downwind: float32 [3, 5, 5], replicated, may hold values from -2.5 to 2.5
- pressure_row: float32 [5], replicated, may hold values from -4 to 4
- face_normal: float32 [3, 128, 256], P(None, 'span', 'chord'), may hold values from -6 to 6
- face_node: int32 [128, 256], P('span', 'chord'), may hold values from 0 to 16383, as said below
- face_count: int32 [16, 2], P('span', 'chord'), may hold values from 128 to 1024, as said below
- adjoint_shell: float32 [6, 16384], P(None, 'span'), may hold values from -6 to 6
- shell_grad: float32 [6, 16384], P(None, 'span'), may hold values from -6 to 6
- node_precond: float32 [6, 6, 16384], P(None, None, 'span'), as said below
- element_stiffness: float32 [24, 24, 4096], P(None, None, ('span', 'chord')), as said below
- connectivity: int32 [4, 4096], P(None, ('span', 'chord')), may hold values from 0 to 16383, as said below
Outputs:
- flow_adjoint: float32 [5, 16, 128, 256], P(None, None, 'span', 'chord')
- shell_adjoint: float32 [6, 16384], P(None, 'span')
Inputs may be any that keep to these rules, and one draw needn't show every extreme that they name: `face_node`: a wall face in the span cells of span index s names a node from max(s - 1, 0) * 1024 to min(s + 2, 16) * 1024 - 1. `face_count`: on each device the wall faces in use are the first ones in span-major, chord-minor order. `connectivity`: the elements of span index s use nodes from s * 1024 to min((s + 1) * 1024 + 64, 16384) - 1. `node_precond`: each node block is near 0.15 times the identity. `element_stiffness`: each element block is symmetric and near the identity.
All inputs are finite; a program needn't handle non-finite values.
Results may differ from a plain program's by a relative error of at most 0.00013.
Values sent between devices are 32-bit elements; how exact they have to be, the bound alone decides.
A program may use at most 64 MiB of HBM per device.

v0:
```python
import functools

import jax
import jax.numpy as jnp
from jax import lax
from jax.experimental import pallas as pl
from jax.experimental.pallas import tpu as pltpu
from jax.sharding import PartitionSpec as P

SW = 4
SS = 3
LANES = 128
ROWS = 8
DEPTH = 3
MESH = pl.DeviceIdType.MESH
F32 = jnp.float32
BF16 = jnp.bfloat16


def split(x):
    lead = x.astype(BF16).astype(F32)
    return jnp.concatenate([lead, x - lead], axis=0).astype(BF16)


def halves(x):
    rows = x.shape[0] // 2
    return x[:rows] + x[rows:]


def dot_nn(a, b):
    return lax.dot_general(a, b, (((1,), (0,)), ((), ())), preferred_element_type=F32)


def dot_nt(a, b):
    return lax.dot_general(a, b, (((1,), (1,)), ((), ())), preferred_element_type=F32)


def flat(tile):
    return jnp.concatenate([tile[r : r + 1] for r in range(tile.shape[0])], axis=1)


def one_hot_lanes(low):
    rows = lax.broadcasted_iota(jnp.int32, (LANES, low.shape[1]), 0)
    return jnp.where(rows == low, 1.0, 0.0).astype(BF16)


def kernel(
    spans, chords, flow, fgrad, diag, coup, upw, dnw, prow, fnorm, fnode, fcount,
    shell0, sgrad, precond, stiff, conn, flow_out, shell_out,
    state, top_s, bot_s, lft_s, rgt_s, top_r, bot_r, lft_r, rgt_r,
    rim_s, rim_r, pt, ptrim, load_s, load_own, load_up, load_dn,
    face_s, face_r, ext_s, ext_r, kv, kv_prev, kv_next, rhs_s, rhs_r,
    ct, ct_r, hot_face, hot_elem, weight, send_sem, recv_sem,
):
    s = lax.axis_index("span")
    c = lax.axis_index("chord")
    layers = flow.shape[1]
    node_dev = shell0.shape[1]
    chunks = node_dev // LANES
    own_rows = ROWS * chunks
    has = {-1: s >= 1, 1: s < spans - 1, -2: s >= 2, 2: s < spans - 2, 0: None}
    hasc = {-1: c >= 1, 1: c < chords - 1, 0: None}

    def both(a, b):
        if a is None:
            return b
        return a if b is None else jnp.logical_and(a, b)

    def when(cond, run):
        if cond is None:
            run()
        else:
            pl.when(cond)(run)

    def mask(cond, x):
        return x if cond is None else jnp.where(cond, x, 0.0)

    barrier = pltpu.get_barrier_semaphore()
    expected = jnp.int32(0)
    for ds in range(-2, 3):
        for k in range(chords):
            if ds == 0 and k == 0:
                continue
            target = (s + ds, lax.rem(c + k, chords))
            when(
                has[ds],
                lambda target=target: pl.semaphore_signal(
                    barrier, inc=1, device_id=target, device_id_type=MESH
                ),
            )
            expected += 1 if ds == 0 else has[ds].astype(jnp.int32)

    ends = []
    used = [0]

    def transfer(src, dst, landing, target, goes, comes):
        i = used[0]
        used[0] += 1

        def make(where):
            return pltpu.make_async_remote_copy(
                src_ref=src, dst_ref=where, send_sem=send_sem.at[i],
                recv_sem=recv_sem.at[i], device_id=target, device_id_type=MESH,
            )

        when(goes, lambda: make(dst).start())
        ends.append(lambda: when(goes, lambda: make(dst).wait_send()))
        return lambda: when(comes, lambda: make(landing).wait_recv())

    def to_span(src, dst, ds):
        return transfer(src, dst, dst, (s + ds, c), has[ds], has[-ds])

    def to_chord(src, dst, dc):
        return transfer(src, dst, dst, (s, c + dc), hasc[dc], hasc[-dc])

    def to_all(src, buf, ds):
        out = []
        for k in range(1 if ds == 0 else 0, chords):
            target = (s + ds, lax.rem(c + k, chords))
            origin = lax.rem(c - k + chords, chords)
            out.append(
                transfer(src, buf.at[c], buf.at[origin], target, has[ds], has[-ds])
            )
        return out

    row = lax.broadcasted_iota(jnp.int32, (ROWS, LANES), 0)
    lane = lax.broadcasted_iota(jnp.int32, (ROWS, LANES), 1)
    zero = jnp.zeros((ROWS, LANES), F32)
    pad2 = jnp.zeros((2, LANES), F32)

    def chunk(ref, h):
        return jnp.concatenate([ref[:, h * LANES : (h + 1) * LANES], pad2], axis=0)

    field = jnp.concatenate([chunk(shell0, h) for h in range(chunks)], axis=0)
    rim_s[...] = field[:ROWS]

    def pack(tile, n, k, j, left, right):
        top_s[k, j, pl.ds(n, 1), :] = tile[0:1]
        bot_s[k, j, pl.ds(n, 1), :] = tile[ROWS - 1 : ROWS]
        left = jnp.where(lane == n, pltpu.roll(tile, n, 1), left)
        right = jnp.where(lane == n, pltpu.roll(tile, n + 1, 1), right)
        return left, right

    def store_packs(k, packs):
        for j in range(5):
            lft_s[k, j] = packs[2 * j]
            rgt_s[k, j] = packs[2 * j + 1]

    def first_edges(n, packs):
        out = []
        for j in range(5):
            out += pack(flow[j, n], n, 0, j, packs[2 * j], packs[2 * j + 1])
        return tuple(out)

    store_packs(0, lax.fori_loop(0, layers, first_edges, (zero,) * 10))

    pl.semaphore_wait(barrier, expected)

    rim_came = to_span(rim_s, rim_r, -1)

    def send_edges(k):
        return [
            to_span(top_s.at[k], top_r.at[k], -1),
            to_span(bot_s.at[k], bot_r.at[k], 1),
            to_chord(lft_s.at[k], lft_r.at[k], -1),
            to_chord(rgt_s.at[k], rgt_r.at[k], 1),
        ]

    edges_came = send_edges(0)

    active = jnp.where(row * LANES + lane < fcount[0, 0], 1.0, 0.0)
    press = prow[0] * flow[0, 0]
    for j in range(1, 5):
        press = press + prow[j] * flow[j, 0]
    press = press * active
    nodes = flat(fnode[...])
    hot_face[1] = one_hot_lanes(jnp.bitwise_and(nodes, LANES - 1))
    own_chunk = jnp.right_shift(nodes - s * node_dev, 7)
    faces = nodes.shape[1]
    rows_f = lax.broadcasted_iota(jnp.int32, (chunks, faces), 0)
    loads = [flat(fnorm[i] * press) for i in range(3)]
    spread = []
    for owner in range(-1, 2):
        here = rows_f + owner * chunks == own_chunk
        for i in range(3):
            spread.append(jnp.where(here, loads[i], 0.0))
    partial = halves(dot_nt(split(jnp.concatenate(spread, axis=0)), hot_face[1]))
    third = 3 * chunks
    for o in range(3):
        load_s[o] = partial[o * third : (o + 1) * third]
    load_own[c] = partial[third : 2 * third]
    loads_came = to_all(load_s.at[1], load_own, 0)
    loads_came += to_all(load_s.at[2], load_up, 1)
    loads_came += to_all(load_s.at[0], load_dn, -1)

    local = conn[...] - s * node_dev
    enode = flat(local)
    echunk = jnp.right_shift(enode, 7)
    hot_elem[...] = one_hot_lanes(jnp.bitwise_and(enode, LANES - 1))
    elems = conn.shape[1]

    def stiffness(field, rim, r):
        table = jnp.concatenate([field, rim], axis=0)
        got = halves(dot_nn(split(table), hot_elem[...]))
        u = jnp.where(echunk == 0, got[:ROWS], 0.0)
        for h in range(1, chunks + 1):
            u = jnp.where(echunk == h, got[h * ROWS : (h + 1) * ROWS], u)
        parts = [None] * 4
        for a in range(4):
            for d in range(6):
                term = stiff[6 * a + d] * u[d : d + 1, a * elems : (a + 1) * elems]
                parts[a] = term if parts[a] is None else parts[a] + term
        f = (parts[0] + parts[1]) + (parts[2] + parts[3])
        force = jnp.concatenate(
            [jnp.concatenate([f[6 * a : 6 * a + 6], pad2], axis=0) for a in range(4)], axis=1
        )
        spread = jnp.concatenate(
            [jnp.where(echunk == h, force, 0.0) for h in range(chunks + 1)], axis=0
        )
        kv[r, c] = halves(dot_nt(split(spread), hot_elem[...]))
        came = to_all(kv.at[r, c], kv.at[r], 0)
        came += to_all(kv.at[r, c, pl.ds(own_rows, ROWS)], kv_prev.at[r], 1)
        if r < SS - 1:
            came += to_all(kv.at[r, c, pl.ds(0, ROWS)], kv_next.at[r], -1)
        return came

    rim_came()
    rim = mask(has[1], rim_r[...])
    kv_came = stiffness(field, rim, 0)

    for d2 in range(6):
        col = jnp.concatenate(
            [precond[d, d2 : d2 + 1, :] for d in range(6)] + [jnp.zeros((2, node_dev), F32)], axis=0
        )
        for h in range(chunks):
            pt[h, d2] = col[:, h * LANES : (h + 1) * LANES]
    pt_came = to_span(pt.at[0], ptrim, -1)

    def total(buf):
        t = buf[0]
        for k in range(1, chords):
            t = t + buf[k]
        return t

    for came in loads_came:
        came()
    load = total(load_own) + mask(has[-1], total(load_up)) + mask(has[1], total(load_dn))
    rhs_rows = []
    for h in range(chunks):
        part = jnp.concatenate(
            [load[i * chunks + h : i * chunks + h + 1] for i in range(3)]
            + [jnp.zeros((ROWS - 3, LANES), F32)], axis=0,
        )
        rhs_rows.append(chunk(sgrad, h) - part)
    rhs = jnp.concatenate(rhs_rows, axis=0)
    rhs_s[...] = rhs[:ROWS]
    rhs_came = to_span(rhs_s, rhs_r, -1)

    node_f = fnode[...].astype(F32)
    for i in range(3):
        face_s[i] = fnorm[i] * active
    face_s[3] = node_f
    faces_came = [to_span(face_s, face_r.at[0], 1), to_span(face_s, face_r.at[1], -1)]
    for n in range(DEPTH):
        for k in range(3):
            ext_s[3 * n + k] = coup[k, n]
        ext_s[3 * DEPTH + n] = 1.0 / diag[n]
    ext_came = []
    for a in range(-1, 2):
        for b in range(-1, 2):
            if a == 0 and b == 0:
                continue
            slot = ext_r.at[a + 1, b + 1]
            ext_came.append(
                transfer(
                    ext_s, slot, slot, (s - a, c - b),
                    both(has[-a], hasc[-b]), both(has[a], hasc[b]),
                )
            )

    def mix(mat, k, tiles):
        out = []
        for i in range(5):
            t = mat[k, i, 0] * tiles[0]
            for j in range(1, 5):
                t = t + mat[k, i, j] * tiles[j]
            out.append(t)
        return out

    def flow_sweep(k, src, dst, came):
        for wait in came:
            wait()

        def body(n, packs):
            above, below = jnp.minimum(n + 1, layers - 1), jnp.maximum(n - 1, 0)
            inv = 1.0 / diag[n]
            acc = [fgrad[j, n] for j in range(5)]
            cur = [src(j, n) for j in range(5)]
            nxt = [jnp.where(n < layers - 1, src(j, above), 0.0) for j in range(5)]
            prv = [jnp.where(n > 0, src(j, below), 0.0) for j in range(5)]
            for d in range(3):
                if d == 0:
                    fwd, bwd = nxt, prv
                elif d == 1:
                    fwd, bwd = [], []
                    for j in range(5):
                        down = mask(has[1], top_r[k, j, pl.ds(n, 1), :])
                        up = mask(has[-1], bot_r[k, j, pl.ds(n, 1), :])
                        fwd.append(jnp.where(row == ROWS - 1, down, pltpu.roll(cur[j], ROWS - 1, 0)))
                        bwd.append(jnp.where(row == 0, up, pltpu.roll(cur[j], 1, 0)))
                else:
                    fwd, bwd = [], []
                    for j in range(5):
                        right = mask(hasc[1], pltpu.roll(lft_r[k, j], LANES - 1 - n, 1))
                        left = mask(hasc[-1], pltpu.roll(rgt_r[k, j], LANES - n, 1))
                        fwd.append(jnp.where(lane == LANES - 1, right, pltpu.roll(cur[j], LANES - 1, 1)))
                        bwd.append(jnp.where(lane == 0, left, pltpu.roll(cur[j], 1, 1)))
                one, two = mix(upw, d, fwd), mix(dnw, d, bwd)
                w = coup[d, n]
                acc = [acc[i] + w * (one[i] + two[i]) for i in range(5)]
            out = []
            for j in range(5):
                tile = inv * acc[j]
                dst(j, n, tile)
                if k < SW - 1:
                    out += pack(tile, n, k + 1, j, packs[2 * j], packs[2 * j + 1])
            return tuple(out)

        packs = lax.fori_loop(0, layers, body, (zero,) * 10 if k < SW - 1 else ())
        if k < SW - 1:
            store_packs(k + 1, packs)
            return send_edges(k + 1)
        return []

    def from_input(j, n):
        return flow[j, n]

    def reader(b):
        return lambda j, n: state[b, j, n]

    def writer(b):
        def put(j, n, tile):
            state[b, j, n] = tile

        return put

    def apply(blocks, res):
        out = blocks(0) * res[0:1]
        for d in range(1, 6):
            out = out + blocks(d) * res[d : d + 1]
        return out

    for r in range(SS):
        edges_came = flow_sweep(
            r, from_input if r == 0 else reader((r + 1) % 2), writer(r % 2), edges_came
        )
        if r == 0:
            for wait in faces_came:
                wait()
            for t in (-1, 0, 1):
                if t == 0:
                    tnodes, normals = nodes, [flat(face_s[i]) for i in range(3)]
                else:
                    got = face_r.at[0 if t == -1 else 1]
                    raw = mask(has[t], got[3]).astype(jnp.int32)
                    tnodes = flat(raw)
                    normals = [flat(mask(has[t], got[i])) for i in range(3)]
                    hot_face[t + 1] = one_hot_lanes(jnp.bitwise_and(tnodes, LANES - 1))
                here = rows_f == jnp.right_shift(tnodes - s * node_dev, 7)
                for i in range(3):
                    weight[t + 1, i] = jnp.where(here, normals[i], 0.0)
            pt_came()
            rhs_came()
            rhs_rim = mask(has[1], rhs_r[...])
        for wait in kv_came:
            wait()
        own = kv[r, 0, pl.ds(0, own_rows), :]
        for k in range(1, chords):
            own = own + kv[r, k, pl.ds(0, own_rows), :]
        spill = mask(has[-1], total(kv_prev.at[r]))
        res = rhs - jnp.concatenate([own[:ROWS] + spill, own[ROWS:]], axis=0)
        if r < SS - 1:
            mine = kv[r, 0, pl.ds(own_rows, ROWS), :]
            for k in range(1, chords):
                mine = mine + kv[r, k, pl.ds(own_rows, ROWS), :]
            res_rim = rhs_rim - (mask(has[1], total(kv_next.at[r])) + mine)
            rim = rim + mask(has[1], apply(lambda d: ptrim[d], res_rim))
        field = field + jnp.concatenate(
            [
                apply(lambda d, h=h: pt[h, d], res[h * ROWS : (h + 1) * ROWS])
                for h in range(chunks)
            ],
            axis=0,
        )
        if r < SS - 1:
            kv_came = stiffness(field, rim, r + 1)

    by_comp = jnp.concatenate(
        [field[h * ROWS + i : h * ROWS + i + 1] for i in range(3) for h in range(chunks)], axis=0
    )
    two = split(by_comp)
    for t in range(3):
        got = halves(dot_nn(two, hot_face[t]))
        acc = weight[t, 0] * got[:chunks]
        for i in range(1, 3):
            acc = acc + weight[t, i] * got[i * chunks : (i + 1) * chunks]
        share = jnp.sum(acc, axis=0, keepdims=True)
        ct[t] = jnp.concatenate(
            [share[:, r * LANES : (r + 1) * LANES] for r in range(ROWS)], axis=0
        )
    ct_came = []
    for ds in range(-2, 3):
        low, high = max(-1, ds - 1) + 1, min(1, ds + 1) + 2
        for dc in range(-1, 2):
            if ds == 0 and dc == 0:
                continue
            piece = pl.ds(low, high - low)
            slot = ct_r.at[2 - ds, 1 - dc, piece]
            ct_came.append(
                transfer(
                    ct.at[piece], slot, slot, (s + ds, c + dc),
                    both(has[ds], hasc[dc]), both(has[-ds], hasc[-dc]),
                )
            )
    for h in range(chunks):
        shell_out[:, h * LANES : (h + 1) * LANES] = field[h * ROWS : h * ROWS + 6]

    def put_out(j, n, tile):
        flow_out[j, n] = tile

    flow_sweep(SW - 1, reader((SW - 2) % 2), put_out, edges_came)

    for wait in ext_came:
        wait()

    def extended(get):
        def at(a, b):
            return get(a, b) if a == 0 and b == 0 else mask(both(has[a], hasc[b]), get(a, b))

        def sides(a):
            return jnp.where(lane < LANES // 2, at(a, 1), at(a, -1))

        upper = jnp.concatenate([at(0, 0), sides(0)], axis=1)
        span_halo = jnp.where(row < ROWS // 2, at(1, 0), at(-1, 0))
        corner = jnp.where(row < ROWS // 2, sides(1), sides(-1))
        return jnp.concatenate([upper, jnp.concatenate([span_halo, corner], axis=1)], axis=0)

    def ext_of(q):
        return extended(lambda a, b: ext_s[q] if a == 0 and b == 0 else ext_r[a + 1, b + 1, q])

    cext = [[ext_of(3 * n + k) for k in range(3)] for n in range(DEPTH)]
    iext = [ext_of(3 * DEPTH + n) for n in range(DEPTH)]

    for wait in ct_came:
        wait()

    def disp_at(tau, dc):
        out = None
        for t in range(-1, 2):
            sigma = tau - t
            if sigma == 0 and dc == 0:
                part = ct[t + 1]
            else:
                part = mask(both(has[sigma], hasc[dc]), ct_r[sigma + 2, dc + 1, t + 1])
            out = part if out is None else out + part
        return out

    disp = extended(disp_at)
    dsrc = [-prow[j] * disp for j in range(5)]

    def crop(x):
        return x[:ROWS, :LANES]

    def add(a, b):
        return b if a is None else [x + y for x, y in zip(a, b)]

    delta = [[iext[0] * dsrc[j] for j in range(5)]]
    for turn in range(1, SW):
        last = turn == SW - 1
        cut = crop if last else (lambda x: x)
        new = []
        for n in range(turn + 1):
            acc = [cut(x) for x in dsrc] if n == 0 else None
            if n < DEPTH:
                cs, inv = [cut(x) for x in cext[n]], cut(iext[n])
            else:
                cs, inv = [coup[k, n] for k in range(3)], 1.0 / diag[n]
            normal = None
            if n + 1 < len(delta):
                normal = mix(upw, 0, [cut(x) for x in delta[n + 1]])
            if n >= 1:
                normal = add(normal, mix(dnw, 0, [cut(x) for x in delta[n - 1]]))
            if normal is not None:
                acc = add(acc, [cs[0] * x for x in normal])
            if n < len(delta):
                here = delta[n]
                for d, axis, size in ((1, 0, 2 * ROWS), (2, 1, 2 * LANES)):
                    fwd = [cut(pltpu.roll(x, size - 1, axis)) for x in here]
                    bwd = [cut(pltpu.roll(x, 1, axis)) for x in here]
                    flux = add(mix(upw, d, fwd), mix(dnw, d, bwd))
                    acc = add(acc, [cs[d] * x for x in flux])
            new.append([inv * x for x in acc])
        delta = new
    for n in range(SW):
        for j in range(5):
            flow_out[j, n] = flow_out[j, n] + delta[n][j]

    for end in ends:
        end()


def per_device(spans, chords, *args):
    flow, node_dev = args[0], args[10].shape[1]
    layers, faces = flow.shape[1], args[8].shape[0] * args[8].shape[1]
    elems = args[14].shape[1]
    chunks = node_dev // LANES
    sems = 43 + 4 * (3 * chords - 1)
    tile = (ROWS, LANES)
    vmem = lambda *shape: pltpu.VMEM(shape, F32)
    span_edge, chord_edge = (SW, 5, layers, LANES), (SW, 5) + tile
    load = (chords, 3 * chunks, LANES)
    quantities = 4 * DEPTH
    table = ROWS * (chunks + 1)
    in_vmem = pl.BlockSpec(memory_space=pltpu.VMEM)
    in_smem = pl.BlockSpec(memory_space=pltpu.SMEM)
    specs = [in_vmem] * 4 + [in_smem] * 3 + [in_vmem] * 2 + [in_smem] + [in_vmem] * 5
    return pl.pallas_call(
        functools.partial(kernel, spans, chords),
        out_shape=(
            jax.ShapeDtypeStruct(flow.shape, F32),
            jax.ShapeDtypeStruct(args[10].shape, F32),
        ),
        in_specs=specs,
        out_specs=(in_vmem, in_vmem),
        scratch_shapes=[
            vmem(2, *flow.shape),
            vmem(*span_edge), vmem(*span_edge), vmem(*chord_edge), vmem(*chord_edge),
            vmem(*span_edge), vmem(*span_edge), vmem(*chord_edge), vmem(*chord_edge),
            vmem(*tile), vmem(*tile),
            vmem(chunks, 6, *tile), vmem(6, *tile),
            vmem(3, 3 * chunks, LANES), vmem(*load), vmem(*load), vmem(*load),
            vmem(4, *tile), vmem(2, 4, *tile),
            vmem(quantities, *tile), vmem(3, 3, quantities, *tile),
            vmem(SS, chords, table, LANES), vmem(SS, chords, *tile), vmem(SS, chords, *tile),
            vmem(*tile), vmem(*tile),
            vmem(3, *tile), vmem(5, 3, 3, *tile),
            pltpu.VMEM((3, LANES, faces), BF16),
            pltpu.VMEM((LANES, 4 * elems), BF16),
            vmem(3, 3, chunks, faces),
            pltpu.SemaphoreType.DMA((sems,)),
            pltpu.SemaphoreType.DMA((sems,)),
        ],
        compiler_params=pltpu.CompilerParams(
            collective_id=0, has_side_effects=True, vmem_limit_bytes=48 * 2**20
        ),
    )(*args)


def solution(mesh):
    spans, chords = mesh.shape["span"], mesh.shape["chord"]
    return jax.shard_map(
        functools.partial(per_device, spans, chords),
        mesh=mesh,
        in_specs=(
            P(None, None, "span", "chord"),
            P(None, None, "span", "chord"),
            P(None, "span", "chord"),
            P(None, None, "span", "chord"),
            P(),
            P(),
            P(),
            P(None, "span", "chord"),
            P("span", "chord"),
            P("span", "chord"),
            P(None, "span"),
            P(None, "span"),
            P(None, None, "span"),
            P(None, None, ("span", "chord")),
            P(None, ("span", "chord")),
        ),
        out_specs=(P(None, None, "span", "chord"), P(None, "span")),
        check_vma=False,
    )
```

profile of v0, /device:TPU:3, one launch (start us, length us, event | category | flops | bytes accessed | tf_op | source)
XLA Modules:
  0.0 40.9 jit_solution(7244890721517252130)
XLA Ops:
  0.6 0.0 copy-start.6
  1.3 0.7 %copy.17.upw = f32[3,5,5]{2,1,0:T(8,128)S(1)} copy(f32[3,5,5]{2,0,1:T(4,128)} %param.19) | data formatting | bytes 600 | tf_op args[4]
  2.0 0.0 copy-start.8
  2.0 0.0 copy-start.11
  2.0 0.7 %copy.18.dnw = f32[3,5,5]{2,1,0:T(8,128)S(1)} copy(f32[3,5,5]{2,0,1:T(4,128)} %param.20) | data formatting | bytes 600 | tf_op args[5]
  2.7 0.0 copy-done.6
  2.7 0.0 copy-done.8
  2.7 0.0 copy-done.11
  2.7 0.0 copy-start
  2.8 1.0 %copy-done = f32[5,16,8,128]{3,2,1,0:T(8,128)S(1)} copy-done((f32[5,16,8,128]{3,2,1,0:T(8,128)S(1)}, f32[5,16,8,128]{3,2,1,0:T(8,128)}, u32[]{:S(2)}) %copy-start) | copy-done | bytes 327704
  3.7 0.0 copy-start.1
  3.7 1.0 %copy-done.1 = f32[5,16,8,128]{3,2,1,0:T(8,128)S(1)} copy-done((f32[5,16,8,128]{3,2,1,0:T(8,128)S(1)}, f32[5,16,8,128]{3,2,1,0:T(8,128)}, u32[]{:S(2)}) %copy-start.1) | copy-done | bytes 327704
  4.7 0.0 copy-start.2
  4.7 1.0 %copy-done.2 = f32[24,24,128]{2,1,0:T(8,128)S(1)} copy-done((f32[24,24,128]{2,1,0:T(8,128)S(1)}, f32[24,24,128]{2,1,0:T(8,128)}, u32[]{:S(2)}) %copy-start.2) | copy-done | bytes 294936
  5.7 0.0 copy-start.3
  5.7 0.9 %copy-done.3 = f32[3,16,8,128]{3,2,1,0:T(8,128)S(1)} copy-done((f32[3,16,8,128]{3,2,1,0:T(8,128)S(1)}, f32[3,16,8,128]{3,2,1,0:T(8,128)}, u32[]{:S(2)}) %copy-start.3) | copy-done | bytes 196632
  6.6 0.0 copy-start.4
  6.6 0.9 %copy-done.4 = f32[6,6,1024]{2,1,0:T(8,128)S(1)} copy-done((f32[6,6,1024]{2,1,0:T(8,128)S(1)}, f32[6,6,1024]{2,1,0:T(8,128)}, u32[]{:S(2)}) %copy-start.4) | copy-done | bytes 147480
  7.5 0.0 copy-start.5
  7.5 0.8 %copy-done.5 = f32[16,8,128]{2,1,0:T(8,128)S(1)} copy-done((f32[16,8,128]{2,1,0:T(8,128)S(1)}, f32[16,8,128]{2,1,0:T(8,128)}, u32[]{:S(2)}) %copy-start.5) | copy-done | bytes 65560
  8.3 0.0 copy-start.7
  8.4 0.8 %copy-done.7 = f32[6,1024]{1,0:T(8,128)S(1)} copy-done((f32[6,1024]{1,0:T(8,128)S(1)}, f32[6,1024]{1,0:T(8,128)}, u32[]{:S(2)}) %copy-start.7) | copy-done | bytes 24600
  9.1 0.0 copy-start.9
  9.1 0.7 %copy-done.9 = s32[8,128]{1,0:T(8,128)S(1)} copy-done((s32[8,128]{1,0:T(8,128)S(1)}, s32[8,128]{1,0:T(8,128)}, u32[]{:S(2)}) %copy-start.9) | copy-done | bytes 4120
  9.8 0.0 copy-start.10
  9.8 0.7 %copy-done.10 = s32[4,128]{1,0:T(4,128)S(1)} copy-done((s32[4,128]{1,0:T(4,128)S(1)}, s32[4,128]{1,0:T(4,128)}, u32[]{:S(2)}) %copy-start.10) | copy-done | bytes 2072
  10.5 29.0 %shard_map.158 = (f32[5,16,8,128]{3,2,1,0:T(8,128)S(1)}, f32[6,1024]{1,0:T(8,128)S(1)}) custom-call(f32[5,16,8,128]{3,2,1,0:T(8,128)S(1)} %copy-done, f32[5,16,8,128]{3,2,1,0:T(8,128)S(1)} %copy-done.1, f32[16,8,128]{2,1,0:T(8,128)S(1)} %copy-done.5, f32[3,16,8,128]{3,2,1,0:T(8,128)S(1)} %copy-done.3, f32[3,5,5]{2,1,0:T(8,128)S(1)} %copy.17.upw, ...), custom_call_target="tpu_custom_call" | custom-call | tf_op jit(solution)/shard_map/pallas_call | solution.py:527
  39.5 0.7 %copy.22 = f32[5,16,8,128]{3,2,1,0:T(8,128)} copy(f32[5,16,8,128]{3,2,1,0:T(8,128)S(1)} %get-tuple-element.4) | data formatting | bytes 655360
  40.3 0.6 %copy.23 = f32[6,1024]{1,0:T(8,128)} copy(f32[6,1024]{1,0:T(8,128)S(1)} %get-tuple-element.5) | data formatting | bytes 49152
Async XLA Ops:
  0.6 2.1 %copy-start.6 = (f32[6,1024]{1,0:T(8,128)S(1)}, f32[6,1024]{1,0:T(8,128)}, u32[]{:S(2)}) copy-start(f32[6,1024]{1,0:T(8,128)} %shell0.1) | copy-start | bytes 73732
  2.0 0.7 %copy-start.8 = (f32[3,8,128]{2,1,0:T(8,128)S(1)}, f32[3,8,128]{2,1,0:T(8,128)}, u32[]{:S(2)}) copy-start(f32[3,8,128]{2,1,0:T(8,128)} %fnorm.1) | copy-start | bytes 36868
  2.0 0.7 %copy-start.11 = (f32[5]{0:T(128)S(1)}, f32[5]{0:T(128)}, u32[]{:S(2)}) copy-start(f32[5]{0:T(128)} %prow.1) | copy-start | bytes 64
  2.7 1.0 %copy-start = (f32[5,16,8,128]{3,2,1,0:T(8,128)S(1)}, f32[5,16,8,128]{3,2,1,0:T(8,128)}, u32[]{:S(2)}) copy-start(f32[5,16,8,128]{3,2,1,0:T(8,128)} %flow.1) | copy-start | bytes 983044
  3.7 1.0 %copy-start.1 = (f32[5,16,8,128]{3,2,1,0:T(8,128)S(1)}, f32[5,16,8,128]{3,2,1,0:T(8,128)}, u32[]{:S(2)}) copy-start(f32[5,16,8,128]{3,2,1,0:T(8,128)} %fgrad.1) | copy-start | bytes 983044
  4.7 1.0 %copy-start.2 = (f32[24,24,128]{2,1,0:T(8,128)S(1)}, f32[24,24,128]{2,1,0:T(8,128)}, u32[]{:S(2)}) copy-start(f32[24,24,128]{2,1,0:T(8,128)} %stiff.1) | copy-start | bytes 884740
  5.7 0.9 %copy-start.3 = (f32[3,16,8,128]{3,2,1,0:T(8,128)S(1)}, f32[3,16,8,128]{3,2,1,0:T(8,128)}, u32[]{:S(2)}) copy-start(f32[3,16,8,128]{3,2,1,0:T(8,128)} %coup.1) | copy-start | bytes 589828
  6.6 0.9 %copy-start.4 = (f32[6,6,1024]{2,1,0:T(8,128)S(1)}, f32[6,6,1024]{2,1,0:T(8,128)}, u32[]{:S(2)}) copy-start(f32[6,6,1024]{2,1,0:T(8,128)} %precond.1) | copy-start | bytes 442372
  7.5 0.8 %copy-start.5 = (f32[16,8,128]{2,1,0:T(8,128)S(1)}, f32[16,8,128]{2,1,0:T(8,128)}, u32[]{:S(2)}) copy-start(f32[16,8,128]{2,1,0:T(8,128)} %diag.1) | copy-start | bytes 196612
  8.3 0.8 %copy-start.7 = (f32[6,1024]{1,0:T(8,128)S(1)}, f32[6,1024]{1,0:T(8,128)}, u32[]{:S(2)}) copy-start(f32[6,1024]{1,0:T(8,128)} %sgrad.1) | copy-start | bytes 73732
  9.1 0.7 %copy-start.9 = (s32[8,128]{1,0:T(8,128)S(1)}, s32[8,128]{1,0:T(8,128)}, u32[]{:S(2)}) copy-start(s32[8,128]{1,0:T(8,128)} %fnode.1) | copy-start | bytes 12292
  9.8 0.7 %copy-start.10 = (s32[4,128]{1,0:T(4,128)S(1)}, s32[4,128]{1,0:T(4,128)}, u32[]{:S(2)}) copy-start(s32[4,128]{1,0:T(4,128)} %conn.1) | copy-start | bytes 6148
where the time goes:
time: 41.5 us; the launch traced here: 40.9 us
  Pallas kernels  29 us (70%)
  local copies, waits for them, and re-layouts  10.5 us (25%)
  between operations  1.32 us (3%)
    pallas_call x1, Pallas kernels, per_device(): pl.pallas_call(functools.partial(kernel, spans, chords), out_shape=(jax.S...  29 us
    unnamed x28, local copies, waits for them, and re-layouts  10.5 us

commit v1 on v0

--- a/solution.py
+++ b/solution.py
@@ -44,14 +44,30 @@
     return jnp.where(rows == low, 1.0, 0.0).astype(BF16)
 
 
-def kernel(
-    spans, chords, flow, fgrad, diag, coup, upw, dnw, prow, fnorm, fnode, fcount,
-    shell0, sgrad, precond, stiff, conn, flow_out, shell_out,
-    state, top_s, bot_s, lft_s, rgt_s, top_r, bot_r, lft_r, rgt_r,
+def kernel(spans, chords, *refs):
+    given, (flow_out, shell_out), local = refs[:15], refs[15:17], refs[17:32]
+    in_sem, rest = refs[32], refs[33:]
+    body(spans, chords, given, local, in_sem, flow_out, shell_out, *rest)
+
+
+def body(
+    spans, chords, given, local, in_sem, flow_out, shell_out, state, top_s, bot_s, lft_s, rgt_s, top_r, bot_r, lft_r, rgt_r,
     rim_s, rim_r, pt, ptrim, load_s, load_own, load_up, load_dn,
     face_s, face_r, ext_s, ext_r, kv, kv_prev, kv_next, rhs_s, rhs_r,
     ct, ct_r, hot_face, hot_elem, weight, send_sem, recv_sem,
 ):
+    loading = [
+        pltpu.make_async_copy(given[i], local[i], in_sem.at[i]) for i in range(len(given))
+    ]
+    for i in (0, 10, 9, 6, 7, 8, 14, 13, 11, 12, 3, 2, 1, 4, 5):
+        loading[i].start()
+    (flow, fgrad, diag, coup, upw, dnw, prow, fnorm, fnode, fcount, shell0, sgrad, precond,
+     stiff, conn) = local
+
+    def need(*which):
+        for i in which:
+            loading[i].wait()
+
     s = lax.axis_index("span")
     c = lax.axis_index("chord")
     layers = flow.shape[1]
@@ -131,6 +147,7 @@
     def chunk(ref, h):
         return jnp.concatenate([ref[:, h * LANES : (h + 1) * LANES], pad2], axis=0)
 
+    need(10)
     field = jnp.concatenate([chunk(shell0, h) for h in range(chunks)], axis=0)
     rim_s[...] = field[:ROWS]
 
@@ -152,6 +169,7 @@
             out += pack(flow[j, n], n, 0, j, packs[2 * j], packs[2 * j + 1])
         return tuple(out)
 
+    need(0)
     store_packs(0, lax.fori_loop(0, layers, first_edges, (zero,) * 10))
 
     pl.semaphore_wait(barrier, expected)
@@ -168,6 +186,7 @@
 
     edges_came = send_edges(0)
 
+    need(9, 6, 7, 8)
     active = jnp.where(row * LANES + lane < fcount[0, 0], 1.0, 0.0)
     press = prow[0] * flow[0, 0]
     for j in range(1, 5):
@@ -193,8 +212,8 @@
     loads_came += to_all(load_s.at[2], load_up, 1)
     loads_came += to_all(load_s.at[0], load_dn, -1)
 
-    local = conn[...] - s * node_dev
-    enode = flat(local)
+    need(14)
+    enode = flat(conn[...] - s * node_dev)
     echunk = jnp.right_shift(enode, 7)
     hot_elem[...] = one_hot_lanes(jnp.bitwise_and(enode, LANES - 1))
     elems = conn.shape[1]
@@ -218,16 +237,17 @@
             [jnp.where(echunk == h, force, 0.0) for h in range(chunks + 1)], axis=0
         )
         kv[r, c] = halves(dot_nt(split(spread), hot_elem[...]))
-        came = to_all(kv.at[r, c], kv.at[r], 0)
-        came += to_all(kv.at[r, c, pl.ds(own_rows, ROWS)], kv_prev.at[r], 1)
+        came = to_all(kv.at[r, c, pl.ds(own_rows, ROWS)], kv_prev.at[r], 1)
         if r < SS - 1:
             came += to_all(kv.at[r, c, pl.ds(0, ROWS)], kv_next.at[r], -1)
-        return came
+        return came + to_all(kv.at[r, c], kv.at[r], 0)
 
     rim_came()
+    need(13)
     rim = mask(has[1], rim_r[...])
     kv_came = stiffness(field, rim, 0)
 
+    need(12, 11)
     for d2 in range(6):
         col = jnp.concatenate(
             [precond[d, d2 : d2 + 1, :] for d in range(6)] + [jnp.zeros((2, node_dev), F32)], axis=0
@@ -256,6 +276,7 @@
     rhs_s[...] = rhs[:ROWS]
     rhs_came = to_span(rhs_s, rhs_r, -1)
 
+    need(3, 2, 1, 4, 5)
     node_f = fnode[...].astype(F32)
     for i in range(3):
         face_s[i] = fnorm[i] * active
@@ -281,9 +302,9 @@
     def mix(mat, k, tiles):
         out = []
         for i in range(5):
-            t = mat[k, i, 0] * tiles[0]
+            t = mat[i, k, 0] * tiles[0]
             for j in range(1, 5):
-                t = t + mat[k, i, j] * tiles[j]
+                t = t + mat[i, k, j] * tiles[j]
             out.append(t)
         return out
 
@@ -291,42 +312,57 @@
         for wait in came:
             wait()
 
-        def body(n, packs):
-            above, below = jnp.minimum(n + 1, layers - 1), jnp.maximum(n - 1, 0)
-            inv = 1.0 / diag[n]
-            acc = [fgrad[j, n] for j in range(5)]
-            cur = [src(j, n) for j in range(5)]
-            nxt = [jnp.where(n < layers - 1, src(j, above), 0.0) for j in range(5)]
-            prv = [jnp.where(n > 0, src(j, below), 0.0) for j in range(5)]
+        group = 2 if layers % 2 == 0 else 1
+
+        def stack(tiles):
+            return jnp.concatenate(tiles, axis=0)
+
+        def around(d, j, n, cur):
+            if d == 0:
+                above, below = jnp.minimum(n + 1, layers - 1), jnp.maximum(n - 1, 0)
+                return (
+                    jnp.where(n < layers - 1, src(j, above), 0.0),
+                    jnp.where(n > 0, src(j, below), 0.0),
+                )
+            if d == 1:
+                down = mask(has[1], top_r[k, j, pl.ds(n, 1), :])
+                up = mask(has[-1], bot_r[k, j, pl.ds(n, 1), :])
+                return (
+                    jnp.where(row == ROWS - 1, down, pltpu.roll(cur, ROWS - 1, 0)),
+                    jnp.where(row == 0, up, pltpu.roll(cur, 1, 0)),
+                )
+            right = mask(hasc[1], pltpu.roll(lft_r[k, j], LANES - 1 - n, 1))
+            left = mask(hasc[-1], pltpu.roll(rgt_r[k, j], LANES - n, 1))
+            return (
+                jnp.where(lane == LANES - 1, right, pltpu.roll(cur, LANES - 1, 1)),
+                jnp.where(lane == 0, left, pltpu.roll(cur, 1, 1)),
+            )
+
+        def body(m, packs):
+            ns = [group * m + g for g in range(group)]
+            cur = [[src(j, n) for n in ns] for j in range(5)]
+            acc = [stack([fgrad[j, n] for n in ns]) for j in range(5)]
             for d in range(3):
-                if d == 0:
-                    fwd, bwd = nxt, prv
-                elif d == 1:
-                    fwd, bwd = [], []
-                    for j in range(5):
-                        down = mask(has[1], top_r[k, j, pl.ds(n, 1), :])
-                        up = mask(has[-1], bot_r[k, j, pl.ds(n, 1), :])
-                        fwd.append(jnp.where(row == ROWS - 1, down, pltpu.roll(cur[j], ROWS - 1, 0)))
-                        bwd.append(jnp.where(row == 0, up, pltpu.roll(cur[j], 1, 0)))
-                else:
-                    fwd, bwd = [], []
-                    for j in range(5):
-                        right = mask(hasc[1], pltpu.roll(lft_r[k, j], LANES - 1 - n, 1))
-                        left = mask(hasc[-1], pltpu.roll(rgt_r[k, j], LANES - n, 1))
-                        fwd.append(jnp.where(lane == LANES - 1, right, pltpu.roll(cur[j], LANES - 1, 1)))
-                        bwd.append(jnp.where(lane == 0, left, pltpu.roll(cur[j], 1, 1)))
+                pairs = [[around(d, j, n, cur[j][g]) for g, n in enumerate(ns)] for j in range(5)]
+                fwd = [stack([p[0] for p in pair]) for pair in pairs]
+                bwd = [stack([p[1] for p in pair]) for pair in pairs]
                 one, two = mix(upw, d, fwd), mix(dnw, d, bwd)
-                w = coup[d, n]
+                w = stack([coup[d, n] for n in ns])
                 acc = [acc[i] + w * (one[i] + two[i]) for i in range(5)]
-            out = []
+            inv = 1.0 / stack([diag[n] for n in ns])
+            packs = list(packs)
             for j in range(5):
-                tile = inv * acc[j]
-                dst(j, n, tile)
-                if k < SW - 1:
-                    out += pack(tile, n, k + 1, j, packs[2 * j], packs[2 * j + 1])
-            return tuple(out)
-
-        packs = lax.fori_loop(0, layers, body, (zero,) * 10 if k < SW - 1 else ())
+                both_tiles = inv * acc[j]
+                for g, n in enumerate(ns):
+                    tile = both_tiles[g * ROWS : (g + 1) * ROWS]
+                    dst(j, n, tile)
+                    if k < SW - 1:
+                        packs[2 * j : 2 * j + 2] = pack(
+                            tile, n, k + 1, j, packs[2 * j], packs[2 * j + 1]
+                        )
+            return tuple(packs)
+
+        packs = lax.fori_loop(0, layers // group, body, (zero,) * 10 if k < SW - 1 else ())
         if k < SW - 1:
             store_packs(k + 1, packs)
             return send_edges(k + 1)
@@ -509,7 +545,24 @@
         end()
 
 
+def hand_on(flow_in, shell_in, flow_out, shell_out, flow_v, shell_v, sem):
+    parts = flow_in.shape[0]
+    inward = [pltpu.make_async_copy(flow_in.at[j], flow_v.at[j], sem.at[0, j]) for j in range(parts)]
+    inward.append(pltpu.make_async_copy(shell_in, shell_v, sem.at[0, parts]))
+    out = [pltpu.make_async_copy(flow_v.at[j], flow_out.at[j], sem.at[1, j]) for j in range(parts)]
+    out.append(pltpu.make_async_copy(shell_v, shell_out, sem.at[1, parts]))
+    for copy in inward:
+        copy.start()
+    for one, two in zip(inward, out):
+        one.wait()
+        two.start()
+    for copy in out:
+        copy.wait()
+
+
 def per_device(spans, chords, *args):
+    turned = [jnp.transpose(args[i], (1, 0, 2)) for i in (4, 5)]
+    args = args[:4] + tuple(turned) + args[6:]
     flow, node_dev = args[0], args[10].shape[1]
     layers, faces = flow.shape[1], args[8].shape[0] * args[8].shape[1]
     elems = args[14].shape[1]
@@ -522,17 +575,22 @@
     quantities = 4 * DEPTH
     table = ROWS * (chunks + 1)
     in_vmem = pl.BlockSpec(memory_space=pltpu.VMEM)
-    in_smem = pl.BlockSpec(memory_space=pltpu.SMEM)
-    specs = [in_vmem] * 4 + [in_smem] * 3 + [in_vmem] * 2 + [in_smem] + [in_vmem] * 5
-    return pl.pallas_call(
+    in_hbm = pl.BlockSpec(memory_space=pltpu.HBM)
+    scalars = (4, 5, 6, 9)
+    kept = [
+        (pltpu.SMEM if i in scalars else pltpu.VMEM)(a.shape, a.dtype) for i, a in enumerate(args)
+    ]
+    results = (
+        jax.ShapeDtypeStruct(flow.shape, F32),
+        jax.ShapeDtypeStruct(args[10].shape, F32),
+    )
+    made = pl.pallas_call(
         functools.partial(kernel, spans, chords),
-        out_shape=(
-            jax.ShapeDtypeStruct(flow.shape, F32),
-            jax.ShapeDtypeStruct(args[10].shape, F32),
-        ),
-        in_specs=specs,
+        out_shape=results,
+        in_specs=[in_hbm] * len(args),
         out_specs=(in_vmem, in_vmem),
-        scratch_shapes=[
+        scratch_shapes=kept + [
+            pltpu.SemaphoreType.DMA((len(args),)),
             vmem(2, *flow.shape),
             vmem(*span_edge), vmem(*span_edge), vmem(*chord_edge), vmem(*chord_edge),
             vmem(*span_edge), vmem(*span_edge), vmem(*chord_edge), vmem(*chord_edge),
@@ -551,9 +609,19 @@
             pltpu.SemaphoreType.DMA((sems,)),
         ],
         compiler_params=pltpu.CompilerParams(
-            collective_id=0, has_side_effects=True, vmem_limit_bytes=48 * 2**20
+            collective_id=0, has_side_effects=True, vmem_limit_bytes=63 * 2**20
         ),
     )(*args)
+    return pl.pallas_call(
+        hand_on,
+        out_shape=results,
+        in_specs=[in_hbm] * 2,
+        out_specs=(in_hbm, in_hbm),
+        scratch_shapes=[
+            pltpu.VMEM(r.shape, F32) for r in results
+        ] + [pltpu.SemaphoreType.DMA((2, flow.shape[0] + 1))],
+        compiler_params=pltpu.CompilerParams(vmem_limit_bytes=63 * 2**20),
+    )(*made)
 
 
 def solution(mesh):

time: 41.5 us -> 29.7 us (0.72)
  local copies, waits for them, and re-layouts: 10.5 us -> 0 us
  Pallas kernels: 29 us -> 27.9 us
    unnamed x28 -> x0, local copies, waits for them, and re-layouts: 10.5 us -> none
    pallas_call x1 -> x2, Pallas kernels: 29 us -> 27.9 us  [the longest x1 26.2 us: per_device(): pl.pallas_call(functools.partial(kernel, spans, chords), out_shape=result...]
where the time goes in v1:
time: 29.7 us; the launch traced here: 29.2 us
  Pallas kernels  27.9 us (94%)
  between operations  1.29 us (4%)
    pallas_call x1, Pallas kernels, per_device(): pl.pallas_call(functools.partial(kernel, spans, chords), out_shape=result...  26.2 us
    pallas_call x1, Pallas kernels, per_device(): pl.pallas_call(hand_on, out_shape=results, in_specs=[in_hbm] * 2, out_spe...  1.71 us

profile of v1, /device:TPU:3, one launch (start us, length us, event | category | flops | bytes accessed | tf_op | source)
XLA Modules:
  0.0 29.2 jit_solution(7383421965407364183)
XLA Ops:
  1.3 26.2 %shard_map.158 = (f32[5,16,8,128]{3,2,1,0:T(8,128)}, f32[6,1024]{1,0:T(8,128)}) custom-call(f32[5,16,8,128]{3,2,1,0:T(8,128)} %refs_0_.1, f32[5,16,8,128]{3,2,1,0:T(8,128)} %refs_1_.1, f32[16,8,128]{2,1,0:T(8,128)} %refs_2_.1, f32[3,16,8,128]{3,2,1,0:T(8,128)} %refs_3_.1, f32[5,3,5]{2,1,0:T(4,128)} %bitcast.2, f32[5,3,5]{2,1,0:T(4,128)} %bitcast.3, ...), custom_call_target="tpu_custom_call" | custom-call | tf_op jit(solution)/shard_map/pallas_call | solution.py:587
  27.5 1.7 %shard_map.159 = (f32[5,16,8,128]{3,2,1,0:T(8,128)}, f32[6,1024]{1,0:T(8,128)}) custom-call(f32[5,16,8,128]{3,2,1,0:T(8,128)} %get-tuple-element.4.flow_in, f32[6,1024]{1,0:T(8,128)} %get-tuple-element.5.shell_in), custom_call_target="tpu_custom_call" | custom-call | tf_op jit(solution)/shard_map/pallas_call | solution.py:615

commit v2 on v1

--- a/solution.py
+++ b/solution.py
@@ -312,7 +312,7 @@
         for wait in came:
             wait()
 
-        group = 2 if layers % 2 == 0 else 1
+        group = next(g for g in (4, 2, 1) if layers % g == 0)
 
         def stack(tiles):
             return jnp.concatenate(tiles, axis=0)

time: 29.7 us -> 28.8 us (0.970)
  Pallas kernels: 27.9 us -> 26.9 us
    pallas_call x1, Pallas kernels: 26.2 us -> 25.2 us  [per_device(): pl.pallas_call(functools.partial(kernel, spans, chords), out_shape=result...]
where the time goes in v2:
time: 28.8 us; the launch traced here: 28.2 us
  Pallas kernels  26.9 us (93%)
  between operations  1.29 us (4%)
    pallas_call x1, Pallas kernels, per_device(): pl.pallas_call(functools.partial(kernel, spans, chords), out_shape=result...  25.2 us
    pallas_call x1, Pallas kernels, per_device(): pl.pallas_call(hand_on, out_shape=results, in_specs=[in_hbm] * 2, out_spe...  1.71 us

profile of v2, /device:TPU:3, one launch (start us, length us, event | category | flops | bytes accessed | tf_op | source)
XLA Modules:
  0.0 28.2 jit_solution(5328478650089651105)
XLA Ops:
  1.3 25.2 %shard_map.158 = (f32[5,16,8,128]{3,2,1,0:T(8,128)}, f32[6,1024]{1,0:T(8,128)}) custom-call(f32[5,16,8,128]{3,2,1,0:T(8,128)} %refs_0_.1, f32[5,16,8,128]{3,2,1,0:T(8,128)} %refs_1_.1, f32[16,8,128]{2,1,0:T(8,128)} %refs_2_.1, f32[3,16,8,128]{3,2,1,0:T(8,128)} %refs_3_.1, f32[5,3,5]{2,1,0:T(4,128)} %bitcast.2, f32[5,3,5]{2,1,0:T(4,128)} %bitcast.3, ...), custom_call_target="tpu_custom_call" | custom-call | tf_op jit(solution)/shard_map/pallas_call | solution.py:587
  26.5 1.7 %shard_map.159 = (f32[5,16,8,128]{3,2,1,0:T(8,128)}, f32[6,1024]{1,0:T(8,128)}) custom-call(f32[5,16,8,128]{3,2,1,0:T(8,128)} %get-tuple-element.4.flow_in, f32[6,1024]{1,0:T(8,128)} %get-tuple-element.5.shell_in), custom_call_target="tpu_custom_call" | custom-call | tf_op jit(solution)/shard_map/pallas_call | solution.py:615
